TPU v7x, 256 devices: a whole 4x4x8 slice. The times are simulated.
256 devices in a mesh: group: 16 (over y_lo, z), expert: 16 (over x, y_hi, core).
Axes of the slice: x: 4, y: 4 (y_hi: 2, y_lo: 2; y = y_hi * 2 + y_lo), z: 8, core: 2. Of those that a mesh axis runs over, the one named last changes fastest.
Arguments:
- train_inputs: float32 [256, 16, 1024], P(('group', 'expert')), as said below
- inv_factor: float32 [256, 1024, 1024], P(('group', 'expert')), as said below
- weights: float32 [256, 1024, 512], P(('group', 'expert')), as said below
- candidates: float32 [16, 4096], replicated, as said below
- test_ids: int32 [1024], replicated, may hold values from 0 to 4095
- basis: bfloat16 [512, 262144], P(None, ('group', 'expert')), may hold values from -0.25 to 0.25
- climatology: float32 [262144], P(('group', 'expert')), may hold values from -3 to 3
Outputs:
- field: bfloat16 [1024, 262144], P(None, ('group', 'expert'))
Inputs may be any that keep to these rules, and one draw needn't show every extreme that they name: inv_factor[e] is lower triangular with L L^T = K + 0.1 I inverted, where K[r, s] = exp(-0.5 |x_r - x_s|^2) over the columns of train_inputs[e]. `train_inputs`: entries of magnitude below 2. `candidates`: entries of magnitude below 2. `weights`: entries of magnitude at most 0.6 * sqrt(256).
All inputs are finite; a program needn't handle non-finite values.
Results may differ from a plain program's by a relative error of at most 0.0045.
Values may be sent and summed in bfloat16 or wider, within the bound.
A program may use at most 64 MiB of HBM per device.

v0:
```python
import jax
import jax.numpy as jnp
from jax import lax
from jax.sharding import PartitionSpec as P

signal_var = 1.0
noise_var = 0.1


def expert_terms(train_points, factor, expert_weights, query_points):
    sq_train = jnp.sum(train_points * train_points, axis=0)
    sq_query = jnp.sum(query_points * query_points, axis=0)
    inner = lax.dot_general(
        train_points,
        query_points,
        (((0,), (0,)), ((), ())),
        precision=lax.Precision.HIGHEST,
        preferred_element_type=jnp.float32,
    )
    cross_kernel = signal_var * jnp.exp(
        -0.5 * (sq_train[:, None] + sq_query[None, :] - 2.0 * inner)
    )
    expert_mean = lax.dot_general(
        cross_kernel,
        expert_weights,
        (((0,), (0,)), ((), ())),
        precision=lax.Precision.HIGHEST,
        preferred_element_type=jnp.float32,
    )
    whitened = jnp.dot(
        factor, cross_kernel, precision=lax.Precision.HIGHEST, preferred_element_type=jnp.float32
    )
    explained = jnp.sum(whitened * whitened, axis=0)
    prior_var = signal_var + noise_var
    post_var = prior_var - explained
    beta_weight = 0.5 * (jnp.log(prior_var) - jnp.log(post_var))
    precision_term = beta_weight / post_var
    return (expert_mean * precision_term[:, None], precision_term, beta_weight)


def body(train_inputs, inv_factor, weights, candidates, test_ids, basis, climatology):
    query_points = jnp.take(candidates, test_ids, axis=1)
    partial_value, weight_term, beta_weight = expert_terms(
        train_inputs[0], inv_factor[0], weights[0], query_points
    )
    prior_var = signal_var + noise_var
    mean_total, weight_total, beta_total = lax.psum(
        (partial_value, weight_term, beta_weight), ("group", "expert")
    )
    precision = weight_total + (1.0 - beta_total) / prior_var
    coefficients = (mean_total / precision[:, None]).astype(jnp.bfloat16)
    field_sum = jnp.dot(coefficients, basis, preferred_element_type=jnp.float32)
    return (field_sum + climatology[None, :]).astype(jnp.bfloat16)


def solution(mesh):
    return jax.shard_map(
        body,
        mesh=mesh,
        in_specs=(
            P(("group", "expert"), None, None),
            P(("group", "expert"), None, None),
            P(("group", "expert"), None, None),
            P(),
            P(),
            P(None, ("group", "expert")),
            P(("group", "expert")),
        ),
        out_specs=P(None, ("group", "expert")),
        check_vma=False,
    )
```

profile of v0, /device:TPU:1, one launch (start us, length us, event | category | flops | bytes accessed | tf_op | source)
XLA Modules:
  0.0 319.7 jit_solution(12277623275109674092)
XLA Ops:
  6.5 0.0 copy-start
  6.5 0.0 copy-start.1
  6.5 0.0 all-reduce.3.cloned.1.call-start
  6.5 0.9 fusion.32
  7.4 0.7 compare_and_fusion
  8.1 2.9 copy.8
  11.0 4.4 %gather_fusion = f32[1024,16]{1,0:T(8,128)S(1)} fusion(f32[16,4096]{0,1:T(8,128)} %copy.8, s32[1024]{0:T(1024)S(1)} %fusion.32), kind=kCustom, calls=%fused_computation | custom fusion | bytes 135168 | tf_op jit(solution)/shard_map/jit(_take)/gather | solution.py:42
  15.4 0.0 copy-start.2
  15.4 0.4 multiply_reduce_fusion.1
  15.7 4.6 %fusion.26 = f32[1024,1024]{1,0:T(8,128)S(1)} fusion(f32[1024,16]{1,0:T(8,128)S(1)} %gather_fusion, pred[1024]{0:T(1024)(128)(4,1)S(1)} %compare_and_fusion, f32[1,16,1024]{2,1,0:T(8,128)} %param.7), kind=kOutput, calls=%fused_computation.22 | convolution fusion | flops 201342976 | bytes 4326400 | tf_op jit(solution)/shard_map/dot_general | solution.py:13
  20.3 0.0 copy-done.1
  20.4 0.0 copy-done.2
  20.4 14.9 %multiply_reduce_fusion = f32[1024]{0:T(1024)S(1)} fusion(f32[1,1024,1024]{2,1,0:T(8,128)S(1)} %copy-done.2, f32[1024,1024]{1,0:T(8,128)S(1)} %fusion.26, f32[1024]{0:T(1024)S(1)} %multiply_reduce_fusion.1, f32[1024]{0:T(1024)S(1)} %fusion.31), kind=kOutput, calls=%fused_computation.7 | convolution fusion | flops 12891192320 | bytes 8400896 | tf_op jit(solution)/shard_map/dot_general | solution.py:30
  35.3 0.0 copy-done
  35.3 0.0 copy-start.3
  35.3 0.0 copy-start.4
  35.3 9.1 %fusion.16 = f32[1024,512]{1,0:T(8,128)} fusion(f32[1,1024,512]{2,1,0:T(8,128)S(1)} %copy-done, f32[1024,1024]{1,0:T(8,128)S(1)} %fusion.26, f32[1024]{0:T(1024)S(1)} %multiply_reduce_fusion.1, f32[1024]{0:T(1024)S(1)} %fusion.31, f32[1024]{0:T(1024)S(1)} %get-tuple-element.8), kind=kOutput, calls=%fused_computation.19 | convolution fusion | flops 6447169536 | bytes 8400896 | tf_op jit(solution)/shard_map/dot_general | solution.py:23
  44.4 0.0 all-reduce.3.cloned.1.call-update
  44.4 82.4 %all-reduce = (f32[1024]{0:T(1024)S(1)}, f32[1024]{0:T(1024)S(1)}) all-reduce(f32[1024]{0:T(1024)S(1)} %get-tuple-element.8, f32[1024]{0:T(1024)S(1)} %get-tuple-element.7), channel_id=1, replica_groups=mesh['group'=16,'expert'=16] {'group','expert'}, use_global_device_ids=true, to_apply=%region_4.5 | all-reduce | flops 2048 | bytes 16384 | tf_op jit(solution)/shard_map/psum | solution.py:47
  126.8 181.7 %all-reduce.3.cloned.1.call-done = f32[1024,512]{1,0:T(8,128)} async-done(((f32[1024,512]{1,0:T(8,128)}), f32[1024,512]{1,0:T(8,128)}) %all-reduce.3.cloned.1.call-update) | async-done | bytes 2097168 | tf_op jit(solution)/shard_map/psum | solution.py:47
  308.6 0.0 copy-done.3
  308.6 0.0 copy-done.4
  308.6 4.2 %add_convert_fusion = bf16[1024,1024]{1,0:T(8,128)(2,1)} fusion(bf16[512,1024]{1,0:T(8,128)(2,1)S(1)} %copy-done.3, f32[1024]{0:T(1024)S(1)} %copy-done.4, f32[1024,512]{1,0:T(8,128)} %all-reduce.3.cloned.1.call-done, f32[1024]{0:T(1024)S(1)} %multiply_add_fusion), kind=kOutput, calls=%fused_computation.6 | convolution fusion | flops 1076887552 | bytes 5251072 | tf_op jit(solution)/shard_map/dot_general | solution.py:52
  (3 shorter events, 0.0 us)
Async XLA Ops:
  6.5 28.8 %copy-start = (f32[1,1024,512]{2,1,0:T(8,128)S(1)}, f32[1,1024,512]{2,1,0:T(8,128)}, u32[]{:S(2)}) copy-start(f32[1,1024,512]{2,1,0:T(8,128)} %param.9) | copy-start | bytes 6291460
  6.5 13.8 %copy-start.1 = (f32[1,16,1024]{2,1,0:T(8,128)S(1)}, f32[1,16,1024]{2,1,0:T(8,128)}, u32[]{:S(2)}) copy-start(f32[1,16,1024]{2,1,0:T(8,128)} %param.7) | copy-start | bytes 196612
  6.5 302.0 %all-reduce.3.cloned.1.call-start = ((), (), s32[]{:S(2)}) async-start(), calls=%async_computation | async-start | bytes 4194304 | tf_op jit(solution)/shard_map/psum | solution.py:47
  15.4 5.0 %copy-start.2 = (f32[1,1024,1024]{2,1,0:T(8,128)S(1)}, f32[1,1024,1024]{2,1,0:T(8,128)}, u32[]{:S(2)}) copy-start(f32[1,1024,1024]{2,1,0:T(8,128)} %param.8) | copy-start | bytes 12582916
  35.3 273.3 %copy-start.3 = (bf16[512,1024]{1,0:T(8,128)(2,1)S(1)}, bf16[512,1024]{1,0:T(8,128)(2,1)}, u32[]{:S(2)}) copy-start(bf16[512,1024]{1,0:T(8,128)(2,1)} %param.12) | copy-start | bytes 3145732
  35.3 273.3 %copy-start.4 = (f32[1024]{0:T(1024)S(1)}, f32[1024]{0:T(1024)}, u32[]{:S(2)}) copy-start(f32[1024]{0:T(1024)} %param.13) | copy-start | bytes 12292
Sparse Core Ops, SparseCore 0:
  44.5 263.9 all-reduce.2
where the time goes:
time: 321 us; the launch traced here: 320 us
  waiting for transfers between devices  182 us (57%)
  blocking collectives  82.4 us (26%)
  matrix products  32.8 us (10%)
  between operations  13.5 us (4%)
  local copies, waits for them, and re-layouts  7.3 us (2%)
    psum x1, waiting for transfers between devices, body(): lax.psum((partial_value, weight_term, beta_weight), ('group', 'expert'))  182 us
    psum x1, blocking collectives, body(): lax.psum((partial_value, weight_term, beta_weight), ('group', 'expert'))  82.4 us
    dot_general x1, matrix products, expert_terms(): jnp.dot(factor, cross_kernel, precision=lax.Precision.HIGHEST, preferred_...  14.9 us
    dot_general x1, matrix products, expert_terms(): lax.dot_general(cross_kernel, expert_weights, (((0,), (0,)), ((), ())), p...  9.08 us
  transfers between devices with their start and end apart: 1, of which 1 were waited for; matrix products, arithmetic and copies ran while one was open for 0% of the time, Pallas kernels for 0%

commit v1 on v0

v1 whole, which is shorter than its diff:
```python
import functools

import jax
import jax.numpy as jnp
from jax import lax
from jax.experimental import pallas as pl
from jax.experimental.pallas import tpu as pltpu
from jax.sharding import PartitionSpec as P

MESH = pl.DeviceIdType.MESH
F32, BF16 = jnp.float32, jnp.bfloat16
PRIOR_VAR = 1.1
TB = 256


def split3(a):
    hi = a.astype(BF16)
    rest = a - hi.astype(F32)
    mid = rest.astype(BF16)
    low = (rest - mid.astype(F32)).astype(BF16)
    return hi, mid, low


def gather_queries(cand_ref, ids_ref, query_ref):
    for tb in range(8):
        ids = jnp.broadcast_to(ids_ref[tb : tb + 1, :], (8, 128))
        lane, block = ids & 127, ids >> 7
        for half in range(2):
            rows = slice(half * 8, half * 8 + 8)
            got = jnp.zeros((8, 128), F32)
            for h in range(32):
                values = jnp.take_along_axis(
                    cand_ref[rows, h * 128 : h * 128 + 128], lane, axis=1, mode="promise_in_bounds"
                )
                got = jnp.where(block == h, values, got)
            query_ref[rows, tb * 128 : tb * 128 + 128] = got


def exponent_sides(query, train):
    qh, qm, ql = split3(query)
    xh, xm, xl = split3(train)
    t = split3(-0.5 * jnp.sum(query * query, axis=0, keepdims=True))
    s = split3(-0.5 * jnp.sum(train * train, axis=0, keepdims=True))
    row = lax.broadcasted_iota(jnp.int32, query.shape, 0)

    def rows(first, parts):
        out = jnp.zeros(query.shape, F32)
        for i, part in enumerate(parts):
            out = jnp.where(row == first + i, part.astype(F32), out)
        return out

    ones = lambda first: jnp.where((row >= first) & (row < first + 3), 1.0, 0.0)
    zero = jnp.zeros(query.shape, BF16)
    left = [qh, qh, qm, qm, qh, ql, (rows(0, t) + ones(3)).astype(BF16), zero]
    right = [xh, xm, xh, xm, xl, xh, (rows(3, s) + ones(0)).astype(BF16), zero]
    return jnp.concatenate(left, 0), jnp.concatenate(right, 0)


def dot_nt(a, b):
    return lax.dot_general(a, b, (((1,), (1,)), ((), ())), preferred_element_type=F32)


def expert_kernel(train_ref, factor_ref, weights_ref, cand_ref, ids_ref, part_ref, q_ref, query_ref, left_ref, right_ref, lb_ref, ll_ref, wb_ref):
    gather_queries(cand_ref, ids_ref, query_ref)
    left, right = exponent_sides(query_ref[...], train_ref[...])
    left_ref[...] = left.T
    right_ref[...] = right
    for b in range(4):
        block = slice(b * 256, b * 256 + 256), slice(0, 256 * (b + 1))
        factor = factor_ref[block]
        high = factor.astype(BF16)
        lb_ref[block] = high
        ll_ref[block] = (factor - high.astype(F32)).astype(BF16)
    wb_ref[...] = weights_ref[...].astype(BF16)
    eye = lax.broadcasted_iota(jnp.int32, (128, 128), 0) == lax.broadcasted_iota(jnp.int32, (128, 128), 1)
    for tb in range(1024 // TB):
        kernel = jnp.exp(jnp.dot(left_ref[tb * TB : tb * TB + TB, :], right_ref[...], preferred_element_type=F32))
        kt = kernel.astype(BF16)
        kl = (kernel - kt.astype(F32)).astype(BF16)
        explained = jnp.zeros((TB, 1), F32)
        for b in range(4):
            block = slice(b * 256, b * 256 + 256), slice(0, 256 * (b + 1))
            whitened = dot_nt(kt[:, block[1]], lb_ref[block])
            whitened += dot_nt(kl[:, block[1]], lb_ref[block])
            whitened += dot_nt(kt[:, block[1]], ll_ref[block])
            explained += jnp.sum(whitened * whitened, axis=1, keepdims=True)
        post_var = PRIOR_VAR - explained
        beta = 0.5 * (jnp.log(jnp.full_like(post_var, PRIOR_VAR)) - jnp.log(post_var))
        term = beta / post_var
        q = term - beta / PRIOR_VAR
        mean = jnp.dot(kt, wb_ref[...], preferred_element_type=F32) * term
        for cb in range(4):
            part_ref[tb * TB // 16 : (tb + 1) * TB // 16, cb] = mean[:, cb * 128 : cb * 128 + 128].reshape(TB // 16, 16, 128)
        for i in range(TB // 128):
            lanes = jnp.sum(jnp.where(eye, q[i * 128 : i * 128 + 128], 0.0), axis=0, keepdims=True)
            q_ref[tb * (TB // 128) + i : tb * (TB // 128) + i + 1, :] = lanes


def place():
    group, expert = lax.axis_index("group"), lax.axis_index("expert")
    return group // 8, group % 8, expert // 4, (expert // 2) % 2, expert % 2


def device(x, y, z, core):
    return ((y % 2) * 8 + z, x * 4 + (y // 2) * 2 + core)


def split_q(q):
    hi = q.astype(BF16).astype(F32)
    return jnp.concatenate([hi, q - hi], 0).astype(BF16)


def join_q(tile):
    tile = tile.astype(F32)
    return tile[:8] + tile[8:]


def sum_kernel(part_ref, q_ref, out_ref, c_recv, x_sum, x_send, x_recv, y_sum, y_recv, z_sum, z_recv,
               tq_send, tq_recv, s_send, s_recv, q_s, q_r, g_s, g_r):
    y_lo, z, x, y_hi, core = place()
    y = y_hi * 2 + y_lo
    peers = (
        [device(x, y, z, 1 - core)]
        + [device((x + d) % 4, y, z, core) for d in (1, 2, 3)]
        + [device(x, (y + d) % 4, z, core) for d in (1, 2, 3)]
        + [device(x, y, (z + d) % 8, core) for d in range(1, 8)]
    )
    barrier = pltpu.get_barrier_semaphore()
    for peer in peers:
        pl.semaphore_signal(barrier, inc=1, device_id=peer, device_id_type=MESH)
    pl.semaphore_wait(barrier, len(peers))

    def send(k, src, dst, gather=False):
        copy = pltpu.make_async_remote_copy(
            src_ref=src, dst_ref=dst,
            send_sem=(g_s if gather else s_send).at[k], recv_sem=(g_r if gather else s_recv).at[k],
            device_id=peers[k], device_id_type=MESH,
        )
        copy.start()
        return copy

    def send_q(k, stage):
        copy = pltpu.make_async_remote_copy(
            src_ref=tq_send.at[stage], dst_ref=tq_recv.at[k], send_sem=q_s.at[k], recv_sem=q_r.at[k],
            device_id=peers[k], device_id_type=MESH,
        )
        copy.start()
        return copy

    started = []
    q = q_ref[...]
    tq_send[0] = split_q(q)
    copies = [send(0, part_ref.at[pl.ds((1 - core) * 32, 32)], c_recv), send_q(0, 0)]
    for c in copies:
        c.wait()
    q += join_q(tq_recv[0])
    x_sum[...] = part_ref[pl.ds(core * 32, 32)] + c_recv[...]

    x_send[...] = x_sum[...].astype(BF16)
    tq_send[1] = split_q(q)
    copies = []
    for i in range(3):
        copies += [send(1 + i, x_send.at[pl.ds(((x + 1 + i) % 4) * 8, 8)], x_recv.at[i]), send_q(1 + i, 1)]
    for c in copies:
        c.wait()
    total = x_sum[pl.ds(x * 8, 8)]
    for i in range(3):
        total += x_recv[i].astype(F32)
        q += join_q(tq_recv[1 + i])
    y_sum[...] = total

    tq_send[2] = split_q(q)
    copies = []
    for i in range(3):
        copies += [send(4 + i, y_sum.at[pl.ds(((y + 1 + i) % 4) * 2, 2)], y_recv.at[i]), send_q(4 + i, 2)]
    for c in copies:
        c.wait()
    total = y_sum[pl.ds(y * 2, 2)]
    for i in range(3):
        total += y_recv[i]
        q += join_q(tq_recv[4 + i])
    z_sum[...] = total

    tq_send[3] = split_q(q)
    copies = []
    for i in range(7):
        to = (z + 1 + i) % 8
        copies += [send(7 + i, z_sum.at[to // 4, to % 4], z_recv.at[i]), send_q(7 + i, 3)]
    for c in copies:
        c.wait()
    total = z_sum[z // 4, z % 4]
    for i in range(7):
        total += z_recv[i]
        q += join_q(tq_recv[7 + i])

    precision = q + 1.0 / PRIOR_VAR
    row = lax.broadcasted_iota(jnp.int32, (8, 128), 0)
    line = jnp.sum(jnp.where(row == core * 4 + x, precision, 0.0), axis=0, keepdims=True)
    pick = lax.broadcasted_iota(jnp.int32, (16, 128), 1) == lax.broadcasted_iota(jnp.int32, (16, 128), 0) + (y * 32 + (z // 4) * 16)
    column = jnp.sum(jnp.where(pick, line, 0.0), axis=1, keepdims=True)

    base_x = (core * 4 + x) * 8
    base_y = base_x + y * 2
    out_ref[base_y + z // 4, z % 4] = (total / column).astype(BF16)
    mine = out_ref.at[base_y + z // 4, z % 4]
    copies = [send(7 + i, mine, mine, True) for i in range(7)]
    for c in copies:
        c.wait()
    mine = out_ref.at[pl.ds(base_y, 2)]
    copies = [send(4 + i, mine, mine, True) for i in range(3)]
    for c in copies:
        c.wait()
    mine = out_ref.at[pl.ds(base_x, 8)]
    copies = [send(1 + i, mine, mine, True) for i in range(3)]
    for c in copies:
        c.wait()
    mine = out_ref.at[pl.ds(core * 32, 32)]
    send(0, mine, mine, True).wait()


def field_kernel(coef_ref, basis_ref, clim_ref, out_ref):
    rows = out_ref.shape[0]
    coef = jnp.concatenate([coef_ref[:, cb].reshape(rows, 128) for cb in range(4)], axis=1)
    out_ref[...] = (jnp.dot(coef, basis_ref[...], preferred_element_type=F32) + clim_ref[...]).astype(BF16)


VM = pl.BlockSpec(memory_space=pltpu.VMEM)


def body(train_inputs, inv_factor, weights, candidates, test_ids, basis, climatology):
    part, q = pl.pallas_call(
        expert_kernel,
        out_shape=(jax.ShapeDtypeStruct((64, 4, 16, 128), F32), jax.ShapeDtypeStruct((8, 128), F32)),
        in_specs=[VM] * 5,
        out_specs=(VM, VM),
        scratch_shapes=[
            pltpu.VMEM((16, 1024), F32),
            pltpu.VMEM((1024, 128), BF16),
            pltpu.VMEM((128, 1024), BF16),
            pltpu.VMEM((1024, 1024), BF16),
            pltpu.VMEM((1024, 1024), BF16),
            pltpu.VMEM((1024, 512), BF16),
        ],
        compiler_params=pltpu.CompilerParams(vmem_limit_bytes=40 << 20),
    )(train_inputs[0], inv_factor[0], weights[0], candidates, test_ids.reshape(8, 128))
    dma = pltpu.SemaphoreType.DMA
    coef = pl.pallas_call(
        sum_kernel,
        out_shape=jax.ShapeDtypeStruct((64, 4, 16, 128), BF16),
        in_specs=[VM] * 2,
        out_specs=VM,
        scratch_shapes=[
            pltpu.VMEM((32, 4, 16, 128), F32),
            pltpu.VMEM((32, 4, 16, 128), F32), pltpu.VMEM((32, 4, 16, 128), BF16), pltpu.VMEM((3, 8, 4, 16, 128), BF16),
            pltpu.VMEM((8, 4, 16, 128), F32), pltpu.VMEM((3, 2, 4, 16, 128), F32),
            pltpu.VMEM((2, 4, 16, 128), F32), pltpu.VMEM((7, 16, 128), F32),
            pltpu.VMEM((4, 16, 128), BF16), pltpu.VMEM((14, 16, 128), BF16),
            dma((14,)), dma((14,)), dma((14,)), dma((14,)), dma((14,)), dma((14,)),
        ],
        compiler_params=pltpu.CompilerParams(collective_id=0, has_side_effects=True, vmem_limit_bytes=24 << 20),
    )(part, q)
    return pl.pallas_call(
        field_kernel,
        out_shape=jax.ShapeDtypeStruct((1024, 1024), BF16),
        grid=(4,),
        in_specs=[
            pl.BlockSpec((16, 4, 16, 128), lambda i: (i, 0, 0, 0)),
            pl.BlockSpec((512, 1024), lambda i: (0, 0)),
            pl.BlockSpec((1, 1024), lambda i: (0, 0)),
        ],
        out_specs=pl.BlockSpec((256, 1024), lambda i: (i, 0)),
        compiler_params=pltpu.CompilerParams(vmem_limit_bytes=24 << 20),
    )(coef, basis, climatology.reshape(1, 1024))


def solution(mesh):
    both = ("group", "expert")
    return jax.shard_map(
        body,
        mesh=mesh,
        in_specs=(P(both, None, None), P(both, None, None), P(both, None, None), P(), P(), P(None, both), P(both)),
        out_specs=P(None, both),
        check_vma=False,
    )
```

time: 321 us -> 65.5 us (0.20)
  waiting for transfers between devices: 182 us -> 0 us
  blocking collectives: 82.4 us -> 0 us
  Pallas kernels: 0 us -> 58.9 us
  matrix products: 32.8 us -> 0 us
  between operations: 13.5 us -> 0.05 us
    psum x1 -> x0, waiting for transfers between devices: 182 us -> none  [body(): lax.psum((partial_value, weight_term, beta_weight), ('group', 'expert'))]
    psum x1 -> x0, blocking collectives: 82.4 us -> none  [body(): lax.psum((partial_value, weight_term, beta_weight), ('group', 'expert'))]
    pallas_call x0 -> x3, Pallas kernels: none -> 58.9 us  [the longest x1 49.6 us: body(): pl.pallas_call(sum_kernel, out_shape=jax.ShapeDtypeStruct((64, 4, 16, 128...]
    dot_general x4 -> x0, matrix products: 32.8 us -> none  [the longest x1 14.9 us: expert_terms(): jnp.dot(factor, cross_kernel, precision=lax.Precision.HIGHEST, preferred_...]
    gather x1 -> x0, local copies, waits for them, and re-layouts: 4.39 us -> none  [body(): query_points = jnp.take(candidates, test_ids, axis=1)]
    unnamed x11 -> x14, local copies, waits for them, and re-layouts: 2.9 us -> 6.27 us
  transfers between devices with their start and end apart: 1 -> 0, of which waited for: 1 -> 0; matrix products, arithmetic and copies ran while one was open for 0% -> 0% of each run, Pallas kernels for 0% -> 0%
where the time goes in v1:
time: 65.5 us; the launch traced here: 65.3 us
  Pallas kernels  58.9 us (90%)
  local copies, waits for them, and re-layouts  6.27 us (10%)
    pallas_call x1, Pallas kernels, body(): pl.pallas_call(sum_kernel, out_shape=jax.ShapeDtypeStruct((64, 4, 16, 128...  49.6 us
    pallas_call x1, Pallas kernels, body(): pl.pallas_call(expert_kernel, out_shape=(jax.ShapeDtypeStruct((64, 4, 16,...  6.38 us
    unnamed x14, local copies, waits for them, and re-layouts  6.27 us
    pallas_call x1, Pallas kernels, body(): pl.pallas_call(field_kernel, out_shape=jax.ShapeDtypeStruct((1024, 1024),...  2.96 us

profile of v1, /device:TPU:1, one launch (start us, length us, event | category | flops | bytes accessed | tf_op | source)
XLA Modules:
  0.0 65.3 jit_solution(5446799348121373599)
XLA Ops:
  0.0 0.0 copy-start
  0.0 2.2 %copy-done = f32[1,1024,1024]{2,1,0:T(8,128)S(1)} copy-done((f32[1,1024,1024]{2,1,0:T(8,128)S(1)}, f32[1,1024,1024]{2,1,0:T(8,128)}, u32[]{:S(2)}) %copy-start) | copy-done | bytes 4194328
  2.2 0.0 copy-start.1
  2.2 1.6 %copy-done.1 = f32[1,1024,512]{2,1,0:T(8,128)S(1)} copy-done((f32[1,1024,512]{2,1,0:T(8,128)S(1)}, f32[1,1024,512]{2,1,0:T(8,128)}, u32[]{:S(2)}) %copy-start.1) | copy-done | bytes 2097176
  3.8 0.0 copy-start.3
  3.8 0.9 %copy-done.3 = f32[16,4096]{1,0:T(8,128)S(1)} copy-done((f32[16,4096]{1,0:T(8,128)S(1)}, f32[16,4096]{1,0:T(8,128)}, u32[]{:S(2)}) %copy-start.3) | copy-done | bytes 262168
  4.7 0.0 copy-start.4
  4.7 0.8 %copy-done.4 = f32[1,16,1024]{2,1,0:T(8,128)S(1)} copy-done((f32[1,16,1024]{2,1,0:T(8,128)S(1)}, f32[1,16,1024]{2,1,0:T(8,128)}, u32[]{:S(2)}) %copy-start.4) | copy-done | bytes 65560
  5.6 0.0 copy-start.6
  5.6 0.7 %copy-done.6 = s32[1024]{0:T(1024)S(1)} copy-done((s32[1024]{0:T(1024)S(1)}, s32[1024]{0:T(1024)}, u32[]{:S(2)}) %copy-start.6) | copy-done | bytes 4120
  6.3 6.4 %shard_map.73 = (f32[64,4,16,128]{3,2,1,0:T(8,128)S(1)}, f32[8,128]{1,0:T(8,128)S(1)}) custom-call(f32[16,1024]{1,0:T(8,128)S(1)} %bitcast.7, f32[1024,1024]{1,0:T(8,128)S(1)} %bitcast.5, f32[1024,512]{1,0:T(8,128)S(1)} %bitcast.6, f32[16,4096]{1,0:T(8,128)S(1)} %copy-done.3, s32[8,128]{1,0:T(8,128)S(1)} %bitcast.9), custom_call_target="tpu_custom_call" | custom-call | tf_op jit(solution)/shard_map/pallas_call | solution.py:231
  12.6 0.0 copy-start.2
  12.7 0.0 copy-start.5
  12.7 49.6 %shard_map.74.coef_ref = bf16[64,4,16,128]{3,2,1,0:T(8,128)(2,1)S(1)} custom-call(f32[64,4,16,128]{3,2,1,0:T(8,128)S(1)} %get-tuple-element.7.part_ref, f32[8,128]{1,0:T(8,128)S(1)} %get-tuple-element.8.q_ref), custom_call_target="tpu_custom_call" | custom-call | tf_op jit(solution)/shard_map/pallas_call | solution.py:247
  62.3 0.0 copy-done.2
  62.3 0.0 copy-done.5
  62.3 3.0 %shard_map.75 = bf16[1024,1024]{1,0:T(8,128)(2,1)} custom-call(bf16[64,4,16,128]{3,2,1,0:T(8,128)(2,1)S(1)} %shard_map.74.coef_ref, bf16[512,1024]{1,0:T(8,128)(2,1)S(1)} %copy-done.2, f32[1,1024]{1,0:T(1,128)S(1)} %bitcast.8), custom_call_target="tpu_custom_call" | custom-call | tf_op jit(solution)/shard_map/pallas_call | solution.py:262
Async XLA Ops:
  0.0 2.2 %copy-start = (f32[1,1024,1024]{2,1,0:T(8,128)S(1)}, f32[1,1024,1024]{2,1,0:T(8,128)}, u32[]{:S(2)}) copy-start(f32[1,1024,1024]{2,1,0:T(8,128)} %param.8) | copy-start | bytes 12582916
  2.2 1.6 %copy-start.1 = (f32[1,1024,512]{2,1,0:T(8,128)S(1)}, f32[1,1024,512]{2,1,0:T(8,128)}, u32[]{:S(2)}) copy-start(f32[1,1024,512]{2,1,0:T(8,128)} %param.9) | copy-start | bytes 6291460
  3.8 0.9 %copy-start.3 = (f32[16,4096]{1,0:T(8,128)S(1)}, f32[16,4096]{1,0:T(8,128)}, u32[]{:S(2)}) copy-start(f32[16,4096]{1,0:T(8,128)} %cand_ref.1) | copy-start | bytes 786436
  4.7 0.8 %copy-start.4 = (f32[1,16,1024]{2,1,0:T(8,128)S(1)}, f32[1,16,1024]{2,1,0:T(8,128)}, u32[]{:S(2)}) copy-start(f32[1,16,1024]{2,1,0:T(8,128)} %param.7) | copy-start | bytes 196612
  5.6 0.7 %copy-start.6 = (s32[1024]{0:T(1024)S(1)}, s32[1024]{0:T(1024)}, u32[]{:S(2)}) copy-start(s32[1024]{0:T(1024)} %param.11) | copy-start | bytes 12292
  12.6 49.6 %copy-start.2 = (bf16[512,1024]{1,0:T(8,128)(2,1)S(1)}, bf16[512,1024]{1,0:T(8,128)(2,1)}, u32[]{:S(2)}) copy-start(bf16[512,1024]{1,0:T(8,128)(2,1)} %basis_ref.1) | copy-start | bytes 3145732
  12.7 49.6 %copy-start.5 = (f32[1024]{0:T(1024)S(1)}, f32[1024]{0:T(1024)}, u32[]{:S(2)}) copy-start(f32[1024]{0:T(1024)} %param.13) | copy-start | bytes 12292

commit v2 on v0

v2 whole, which is shorter than its diff:
```python
import functools

import jax
import jax.numpy as jnp
from jax import lax
from jax.experimental import pallas as pl
from jax.experimental.pallas import tpu as pltpu
from jax.sharding import PartitionSpec as P

MESH = pl.DeviceIdType.MESH
F32, BF16 = jnp.float32, jnp.bfloat16
PRIOR_VAR = 1.1
TB = 256
PLANE = [(dx, dy) for dx in range(4) for dy in range(4) if dx or dy]
PLANE.sort(key=lambda d: -(min(d[0], 4 - d[0]) + min(d[1], 4 - d[1])))
ALONG = [4, 3, 5, 2, 6, 1, 7]


def split3(a):
    hi = a.astype(BF16)
    rest = a - hi.astype(F32)
    mid = rest.astype(BF16)
    low = (rest - mid.astype(F32)).astype(BF16)
    return hi, mid, low


def gather_queries(cand_ref, ids_ref, query_ref):
    for tb in range(8):
        ids = jnp.broadcast_to(ids_ref[tb : tb + 1, :], (8, 128))
        lane, block = ids & 127, ids >> 7
        for half in range(2):
            rows = slice(half * 8, half * 8 + 8)
            got = jnp.zeros((8, 128), F32)
            for h in range(32):
                values = jnp.take_along_axis(
                    cand_ref[rows, h * 128 : h * 128 + 128], lane, axis=1, mode="promise_in_bounds"
                )
                got = jnp.where(block == h, values, got)
            query_ref[rows, tb * 128 : tb * 128 + 128] = got


def exponent_sides(query, train):
    qh, qm, ql = split3(query)
    xh, xm, xl = split3(train)
    t = split3(-0.5 * jnp.sum(query * query, axis=0, keepdims=True))
    s = split3(-0.5 * jnp.sum(train * train, axis=0, keepdims=True))
    row = lax.broadcasted_iota(jnp.int32, query.shape, 0)

    def rows(first, parts):
        out = jnp.zeros(query.shape, F32)
        for i, part in enumerate(parts):
            out = jnp.where(row == first + i, part.astype(F32), out)
        return out

    ones = lambda first: jnp.where((row >= first) & (row < first + 3), 1.0, 0.0)
    zero = jnp.zeros(query.shape, BF16)
    left = [qh, qh, qm, qm, qh, ql, (rows(0, t) + ones(3)).astype(BF16), zero]
    right = [xh, xm, xh, xm, xl, xh, (rows(3, s) + ones(0)).astype(BF16), zero]
    return jnp.concatenate(left, 0), jnp.concatenate(right, 0)


def dot_nt(a, b):
    return lax.dot_general(a, b, (((1,), (1,)), ((), ())), preferred_element_type=F32)


def place():
    group, expert = lax.axis_index("group"), lax.axis_index("expert")
    return group // 8, group % 8, expert // 4, (expert // 2) % 2, expert % 2


def device(x, y, z, core):
    return ((y % 2) * 8 + z, x * 4 + (y // 2) * 2 + core)


def split_q(q):
    hi = q.astype(BF16).astype(F32)
    return jnp.concatenate([hi, q - hi], 0).astype(BF16)


def join_q(tile):
    tile = tile.astype(F32)
    return tile[:8] + tile[8:]


def tiles(a):
    return jnp.stack([a[:, cb * 128 : cb * 128 + 128].reshape(-1, 16, 128) for cb in range(4)], axis=1)


def rows_of(t):
    return jnp.concatenate([t[:, cb].reshape(-1, 128) for cb in range(4)], axis=1)


def main_kernel(train_hbm, cand_hbm, ids_hbm, factor_ref, weights_ref, basis_ref, clim_hbm, out_ref,
                train_ref, cand_ref, ids_ref, query_ref, left_ref, right_ref, lf, lb, ll, wf, wb, basis_v, clim_ref, kh, kl, term_ref, q_ref,
                c_send, c_recv, own, p_send0, p_send1, p_recv0, p_recv1, z_send, z_recv, z_own, coef,
                i_sem, l_sem, w_sem, b_sem, m_sem, c_s, c_r, p_s, p_r, z_s, z_r, g_s, g_r, h_s, h_r):
    y_lo, z, x, y_hi, core = place()
    y = y_hi * 2 + y_lo
    plane = x * 4 + y
    partner = device(x, y, z, 1 - core)
    plane_peers = [device((x + dx) % 4, (y + dy) % 4, z, core) for dx, dy in PLANE]
    z_peers = [device(x, y, (z + d) % 8, core) for d in ALONG]

    copies = [
        pltpu.make_async_copy(ids_hbm, ids_ref, i_sem.at[0]),
        pltpu.make_async_copy(cand_hbm, cand_ref, i_sem.at[1]),
        pltpu.make_async_copy(train_hbm, train_ref, i_sem.at[2]),
    ]
    for copy in copies:
        copy.start()
    l_copies = []
    for b in range(4):
        block = pl.ds(b * 256, 256), pl.ds(0, 256 * (b + 1))
        l_copies.append(pltpu.make_async_copy(factor_ref.at[block], lf.at[block], l_sem.at[b]))
    w_copy = pltpu.make_async_copy(weights_ref, wf, w_sem)
    m_copy = pltpu.make_async_copy(clim_hbm, clim_ref, m_sem)
    b_copy = pltpu.make_async_copy(basis_ref, basis_v, b_sem)
    for copy in l_copies:
        copy.start()
    w_copy.start()
    b_copy.start()
    m_copy.start()

    barrier = pltpu.get_barrier_semaphore()
    everyone = [partner] + plane_peers + z_peers
    for peer in everyone:
        pl.semaphore_signal(barrier, inc=1, device_id=peer, device_id_type=MESH)

    def send(src, dst, s_sem, r_sem, peer):
        copy = pltpu.make_async_remote_copy(
            src_ref=src, dst_ref=dst, send_sem=s_sem, recv_sem=r_sem, device_id=peer, device_id_type=MESH
        )
        copy.start()
        return copy

    for copy in copies:
        copy.wait()
    gather_queries(cand_ref, ids_ref, query_ref)
    left, right = exponent_sides(query_ref[...], train_ref[...])
    left_ref[...] = left.T
    right_ref[...] = right

    @pl.loop(0, 4)
    def _(tb):
        rows = pl.ds(pl.multiple_of(tb * TB, TB), TB)
        kernel = jnp.exp(jnp.dot(left_ref[rows, :], right_ref[...], preferred_element_type=F32))
        high = kernel.astype(BF16)
        kh[rows, :] = high
        kl[rows, :] = (kernel - high.astype(F32)).astype(BF16)

    for b in range(4):
        l_copies[b].wait()
        block = slice(b * 256, b * 256 + 256), slice(0, 256 * (b + 1))
        factor = lf[block]
        high = factor.astype(BF16)
        lb[block] = high
        ll[block] = (factor - high.astype(F32)).astype(BF16)

    eye = lax.broadcasted_iota(jnp.int32, (128, 128), 0) == lax.broadcasted_iota(jnp.int32, (128, 128), 1)

    @pl.loop(0, 4)
    def _(tb):
        rows = pl.ds(pl.multiple_of(tb * TB, TB), TB)
        explained = jnp.zeros((TB, 1), F32)
        for b in range(4):
            block = slice(b * 256, b * 256 + 256), slice(0, 256 * (b + 1))
            whitened = dot_nt(kh[rows, block[1]], lb[block])
            whitened += dot_nt(kl[rows, block[1]], lb[block])
            whitened += dot_nt(kh[rows, block[1]], ll[block])
            explained += jnp.sum(whitened * whitened, axis=1, keepdims=True)
        post_var = PRIOR_VAR - explained
        beta = 0.5 * (jnp.log(jnp.full_like(post_var, PRIOR_VAR)) - jnp.log(post_var))
        term = beta / post_var
        term_ref[rows, :] = term
        q = term - beta / PRIOR_VAR
        for i in range(TB // 128):
            lanes = jnp.sum(jnp.where(eye, q[i * 128 : i * 128 + 128], 0.0), axis=0, keepdims=True)
            q_ref[pl.ds(tb * (TB // 128) + i, 1), :] = lanes

    w_copy.wait()
    wb[...] = wf[...].astype(BF16)

    def mean(block):
        rows = pl.ds(pl.multiple_of(block * TB, TB), TB)
        return tiles(jnp.dot(kh[rows, :], wb[...], preferred_element_type=F32) * term_ref[rows, :])

    q = q_ref[...]
    c_send[0, 64, :8] = q
    c_send[0, 64, 8:] = q
    core_copies = []
    for g in range(2):
        c_send[g, :64] = mean(g * 2 + 1 - core).reshape(64, 16, 128)
        if g == 0:
            pl.semaphore_wait(barrier, len(everyone))
        n = 65 if g == 0 else 64
        core_copies.append(send(c_send.at[g, pl.ds(0, n)], c_recv.at[g, pl.ds(0, n)], c_s.at[g], c_r.at[g], partner))

    plane_copies = [[], []]
    for g in range(2):
        mine = mean(g * 2 + core)
        core_copies[g].wait()
        mine += c_recv[g, :64].reshape(16, 4, 16, 128)
        own[g] = mine
        p_send, p_recv = (p_send0, p_recv0) if g == 0 else (p_send1, p_recv1)
        p_send[:, :4] = mine.astype(BF16)
        if g == 0:
            q += c_recv[0, 64, :8]
            p_send[:, 4] = jnp.broadcast_to(split_q(q)[None], (16, 16, 128))
        for k, (dx, dy) in enumerate(PLANE):
            to = ((x + dx) % 4) * 4 + (y + dy) % 4
            plane_copies[g].append(send(p_send.at[to], p_recv.at[k], p_s.at[g, k], p_r.at[g, k], plane_peers[k]))

    z_copies = [[], []]
    for g in range(2):
        p_recv = p_recv0 if g == 0 else p_recv1
        total = own[g, plane]
        for k in range(15):
            plane_copies[g][k].wait()
            total += p_recv[k, :4].astype(F32)
            if g == 0:
                q += join_q(p_recv[k, 4])
        z_own[g] = total
        z_send[g, :4] = total.astype(BF16)
        if g == 0:
            z_send[0, 4] = split_q(q)
        n = 5 if g == 0 else 4
        for k in range(7):
            z_copies[g].append(send(z_send.at[g, pl.ds(0, n)], z_recv.at[g, k, pl.ds(0, n)], z_s.at[g, k], z_r.at[g, k], z_peers[k]))

    row = lax.broadcasted_iota(jnp.int32, (8, 128), 0)
    pick_row = lax.broadcasted_iota(jnp.int32, (16, 128), 0) + (plane % 8) * 16
    pick = lax.broadcasted_iota(jnp.int32, (16, 128), 1) == pick_row
    gather_copies = [[], []]
    for g in range(2):
        total = z_own[g]
        for k in range(7):
            z_copies[g][k].wait()
            total += z_recv[g, k, :4].astype(F32)
            if g == 0:
                q += join_q(z_recv[0, k, 4])
        if g == 0:
            precision = q + 1.0 / PRIOR_VAR
        line = jnp.sum(jnp.where(row == (g * 2 + core) * 2 + plane // 8, precision, 0.0), axis=0, keepdims=True)
        column = jnp.sum(jnp.where(pick, line, 0.0), axis=1, keepdims=True)
        spot = (g * 2 + core) * 16 + plane
        coef[spot] = (total / column).astype(BF16)
        for k in range(15):
            gather_copies[g].append(send(coef.at[spot], coef.at[spot], g_s.at[g, k], g_r.at[g, k], plane_peers[k]))

    b_copy.wait()
    m_copy.wait()

    def field(block):
        c = rows_of(coef[pl.ds(block * 16, 16)])
        rows = pl.ds(pl.multiple_of(block * TB, TB), TB)
        out_ref[rows, :] = (jnp.dot(c, basis_v[...], preferred_element_type=F32) + clim_ref[...]).astype(BF16)

    last = []
    for g in range(2):
        for k in range(15):
            gather_copies[g][k].wait()
        half = coef.at[pl.ds((g * 2 + core) * 16, 16)]
        last.append(send(half, half, h_s.at[g], h_r.at[g], partner))
    field(core)
    last[0].wait()
    field(1 - core)
    field(2 + core)
    last[1].wait()
    field(3 - core)


VM = pl.BlockSpec(memory_space=pltpu.VMEM)
HBM = pl.BlockSpec(memory_space=pltpu.HBM)


def body(train_inputs, inv_factor, weights, candidates, test_ids, basis, climatology):
    arrays = train_inputs[0], candidates, test_ids.reshape(8, 128), inv_factor[0], weights[0], basis, climatology.reshape(1, 1024)
    dma = pltpu.SemaphoreType.DMA
    tile = lambda *n: pltpu.VMEM((*n, 16, 128), BF16)
    tile32 = lambda *n: pltpu.VMEM((*n, 16, 128), F32)
    return pl.pallas_call(
        main_kernel,
        out_shape=jax.ShapeDtypeStruct((1024, 1024), BF16),
        in_specs=[HBM] * 7,
        out_specs=VM,
        scratch_shapes=[
            pltpu.VMEM((16, 1024), F32), pltpu.VMEM((16, 4096), F32), pltpu.VMEM((8, 128), jnp.int32), pltpu.VMEM((16, 1024), F32),
            pltpu.VMEM((1024, 128), BF16), pltpu.VMEM((128, 1024), BF16),
            pltpu.VMEM((1024, 1024), F32), pltpu.VMEM((1024, 1024), BF16), pltpu.VMEM((1024, 1024), BF16),
            pltpu.VMEM((1024, 512), F32), pltpu.VMEM((1024, 512), BF16), pltpu.VMEM((512, 1024), BF16), pltpu.VMEM((1, 1024), F32),
            pltpu.VMEM((1024, 1024), BF16), pltpu.VMEM((1024, 1024), BF16),
            pltpu.VMEM((1024, 1), F32), pltpu.VMEM((8, 128), F32),
            tile32(2, 65), tile32(2, 65), tile32(2, 16, 4),
            tile(16, 5), tile(16, 4), tile(15, 5), tile(15, 4), tile(2, 5), tile(2, 7, 5), tile32(2, 4), tile(64, 4),
            dma((3,)), dma((4,)), dma, dma, dma, dma((2,)), dma((2,)), dma((2, 15)), dma((2, 15)), dma((2, 7)), dma((2, 7)),
            dma((2, 15)), dma((2, 15)), dma((2,)), dma((2,)),
        ],
        compiler_params=pltpu.CompilerParams(collective_id=0, has_side_effects=True, vmem_limit_bytes=44 << 20),
    )(*[pltpu.with_memory_space_constraint(a, pltpu.HBM) for a in arrays])


def solution(mesh):
    both = ("group", "expert")
    return jax.shard_map(
        body,
        mesh=mesh,
        in_specs=(P(both, None, None), P(both, None, None), P(both, None, None), P(), P(), P(None, both), P(both)),
        out_specs=P(None, both),
        check_vma=False,
    )
```

time: 321 us -> 45.4 us (0.14)
  waiting for transfers between devices: 182 us -> 0 us
  blocking collectives: 82.4 us -> 0 us
  Pallas kernels: 0 us -> 44 us
  matrix products: 32.8 us -> 0 us
  between operations: 13.5 us -> 0.01 us
  local copies, waits for them, and re-layouts: 7.3 us -> 1.32 us
    psum x1 -> x0, waiting for transfers between devices: 182 us -> none  [body(): lax.psum((partial_value, weight_term, beta_weight), ('group', 'expert'))]
    psum x1 -> x0, blocking collectives: 82.4 us -> none  [body(): lax.psum((partial_value, weight_term, beta_weight), ('group', 'expert'))]
    pallas_call x0 -> x1, Pallas kernels: none -> 44 us  [body(): pl.pallas_call(main_kernel, out_shape=jax.ShapeDtypeStruct((1024, 1024),...]
    dot_general x4 -> x0, matrix products: 32.8 us -> none  [the longest x1 14.9 us: expert_terms(): jnp.dot(factor, cross_kernel, precision=lax.Precision.HIGHEST, preferred_...]
    gather x1 -> x0, local copies, waits for them, and re-layouts: 4.39 us -> none  [body(): query_points = jnp.take(candidates, test_ids, axis=1)]
  transfers between devices with their start and end apart: 1 -> 0, of which waited for: 1 -> 0; matrix products, arithmetic and copies ran while one was open for 0% -> 0% of each run, Pallas kernels for 0% -> 0%
where the time goes in v2:
time: 45.4 us; the launch traced here: 45.3 us
  Pallas kernels  44 us (97%)
  local copies, waits for them, and re-layouts  1.32 us (3%)
    pallas_call x1, Pallas kernels, body(): pl.pallas_call(main_kernel, out_shape=jax.ShapeDtypeStruct((1024, 1024),...  44 us
    unnamed x1, local copies, waits for them, and re-layouts  1.32 us

profile of v2, /device:TPU:1, one launch (start us, length us, event | category | flops | bytes accessed | tf_op | source)
XLA Modules:
  0.0 45.3 jit_solution(2660885533178712104)
XLA Ops:
  0.0 44.0 %shard_map.73 = bf16[1024,1024]{1,0:T(8,128)(2,1)S(1)} custom-call(f32[16,1024]{1,0:T(8,128)} %bitcast.7, f32[16,4096]{1,0:T(8,128)} %cand_hbm.1, s32[8,128]{1,0:T(8,128)} %bitcast.8, f32[1024,1024]{1,0:T(8,128)} %bitcast.5, f32[1024,512]{1,0:T(8,128)} %bitcast.6, bf16[512,1024]{1,0:T(8,128)(2,1)} %basis_ref.1, f32[1,1024]{1,0:T(1,128)} %bitcast.9), custom_call_target="tpu_custom_call" | custom-call | tf_op jit(solution)/shard_map/pallas_call | solution.py:281
  44.0 1.3 %copy.9 = bf16[1024,1024]{1,0:T(8,128)(2,1)} copy(bf16[1024,1024]{1,0:T(8,128)(2,1)S(1)} %shard_map.73) | data formatting | bytes 4194304

commit v3 on v2

--- a/solution.py
+++ b/solution.py
@@ -10,7 +10,7 @@
 MESH = pl.DeviceIdType.MESH
 F32, BF16 = jnp.float32, jnp.bfloat16
 PRIOR_VAR = 1.1
-TB = 256
+NK = 2
 PLANE = [(dx, dy) for dx in range(4) for dy in range(4) if dx or dy]
 PLANE.sort(key=lambda d: -(min(d[0], 4 - d[0]) + min(d[1], 4 - d[1])))
 ALONG = [4, 3, 5, 2, 6, 1, 7]
@@ -92,7 +92,7 @@
 
 def main_kernel(train_hbm, cand_hbm, ids_hbm, factor_ref, weights_ref, basis_ref, clim_hbm, out_ref,
                 train_ref, cand_ref, ids_ref, query_ref, left_ref, right_ref, lf, lb, ll, wf, wb, basis_v, clim_ref, kh, kl, term_ref, q_ref,
-                c_send, c_recv, own, p_send0, p_send1, p_recv0, p_recv1, z_send, z_recv, z_own, coef,
+                c_send, c_recv, own, p_send0, p_send, p_recv0, p_recv, z_send, z_recv0, z_recv, z_own, coef,
                 i_sem, l_sem, w_sem, b_sem, m_sem, c_s, c_r, p_s, p_r, z_s, z_r, g_s, g_r, h_s, h_r):
     y_lo, z, x, y_hi, core = place()
     y = y_hi * 2 + y_lo
@@ -117,9 +117,6 @@
     b_copy = pltpu.make_async_copy(basis_ref, basis_v, b_sem)
     for copy in l_copies:
         copy.start()
-    w_copy.start()
-    b_copy.start()
-    m_copy.start()
 
     barrier = pltpu.get_barrier_semaphore()
     everyone = [partner] + plane_peers + z_peers
@@ -133,140 +130,149 @@
         copy.start()
         return copy
 
+    def wait_all(like, s_sem, r_sem, peer):
+        pltpu.make_async_remote_copy(
+            src_ref=like, dst_ref=like, send_sem=s_sem, recv_sem=r_sem, device_id=peer, device_id_type=MESH
+        ).wait()
+
     for copy in copies:
         copy.wait()
     gather_queries(cand_ref, ids_ref, query_ref)
     left, right = exponent_sides(query_ref[...], train_ref[...])
     left_ref[...] = left.T
     right_ref[...] = right
-
-    @pl.loop(0, 4)
-    def _(tb):
-        rows = pl.ds(pl.multiple_of(tb * TB, TB), TB)
+    w_copy.start()
+
+    def cross(tb):
+        rows = slice(tb * 256, tb * 256 + 256)
         kernel = jnp.exp(jnp.dot(left_ref[rows, :], right_ref[...], preferred_element_type=F32))
         high = kernel.astype(BF16)
         kh[rows, :] = high
         kl[rows, :] = (kernel - high.astype(F32)).astype(BF16)
 
+    def explain(tb):
+        rows = slice(tb * 256, tb * 256 + 256)
+        squares = jnp.zeros((256, 128), F32)
+        for b in range(4):
+            block = slice(b * 256, b * 256 + 256), slice(0, 256 * (b + 1))
+            whitened = dot_nt(kh[rows, block[1]], lb[block])
+            whitened += dot_nt(kl[rows, block[1]], lb[block])
+            whitened += dot_nt(kh[rows, block[1]], ll[block])
+            squares += whitened[:, :128] * whitened[:, :128] + whitened[:, 128:] * whitened[:, 128:]
+        explained = jnp.sum(squares, axis=1, keepdims=True)
+        post_var = PRIOR_VAR - explained
+        beta = 0.5 * (jnp.log(jnp.full_like(post_var, PRIOR_VAR)) - jnp.log(post_var))
+        term = beta / post_var
+        term_ref[rows, :] = term
+        q = term - beta / PRIOR_VAR
+        for i in range(2):
+            lanes = jnp.sum(jnp.where(eye, q[i * 128 : i * 128 + 128], 0.0), axis=0, keepdims=True)
+            q_ref[tb * 2 + i : tb * 2 + i + 1, :] = lanes
+
+    eye = lax.broadcasted_iota(jnp.int32, (128, 128), 0) == lax.broadcasted_iota(jnp.int32, (128, 128), 1)
+    for tb in range(NK):
+        cross(tb)
+    for copy in l_copies:
+        copy.wait()
     for b in range(4):
-        l_copies[b].wait()
         block = slice(b * 256, b * 256 + 256), slice(0, 256 * (b + 1))
         factor = lf[block]
         high = factor.astype(BF16)
         lb[block] = high
         ll[block] = (factor - high.astype(F32)).astype(BF16)
-
-    eye = lax.broadcasted_iota(jnp.int32, (128, 128), 0) == lax.broadcasted_iota(jnp.int32, (128, 128), 1)
-
-    @pl.loop(0, 4)
-    def _(tb):
-        rows = pl.ds(pl.multiple_of(tb * TB, TB), TB)
-        explained = jnp.zeros((TB, 1), F32)
-        for b in range(4):
-            block = slice(b * 256, b * 256 + 256), slice(0, 256 * (b + 1))
-            whitened = dot_nt(kh[rows, block[1]], lb[block])
-            whitened += dot_nt(kl[rows, block[1]], lb[block])
-            whitened += dot_nt(kh[rows, block[1]], ll[block])
-            explained += jnp.sum(whitened * whitened, axis=1, keepdims=True)
-        post_var = PRIOR_VAR - explained
-        beta = 0.5 * (jnp.log(jnp.full_like(post_var, PRIOR_VAR)) - jnp.log(post_var))
-        term = beta / post_var
-        term_ref[rows, :] = term
-        q = term - beta / PRIOR_VAR
-        for i in range(TB // 128):
-            lanes = jnp.sum(jnp.where(eye, q[i * 128 : i * 128 + 128], 0.0), axis=0, keepdims=True)
-            q_ref[pl.ds(tb * (TB // 128) + i, 1), :] = lanes
+    for tb in range(4):
+        if tb + NK < 4:
+            cross(tb + NK)
+        explain(tb)
 
     w_copy.wait()
+    b_copy.start()
+    m_copy.start()
     wb[...] = wf[...].astype(BF16)
 
-    def mean(block):
-        rows = pl.ds(pl.multiple_of(block * TB, TB), TB)
-        return tiles(jnp.dot(kh[rows, :], wb[...], preferred_element_type=F32) * term_ref[rows, :])
-
     q = q_ref[...]
-    c_send[0, 64, :8] = q
-    c_send[0, 64, 8:] = q
     core_copies = []
-    for g in range(2):
-        c_send[g, :64] = mean(g * 2 + 1 - core).reshape(64, 16, 128)
+    for g in range(4):
+        rows = slice(g * 256, g * 256 + 256)
+        mean = jnp.dot(kh[rows, :], wb[...], preferred_element_type=F32) * term_ref[rows, :]
+        c_send[g, :, :32] = tiles(mean).reshape(2, 32, 16, 128)
+        n = 32
         if g == 0:
+            n = 33
+            c_send[0, :, 32] = jnp.broadcast_to(jnp.concatenate([q, q], 0)[None], (2, 16, 128))
             pl.semaphore_wait(barrier, len(everyone))
-        n = 65 if g == 0 else 64
-        core_copies.append(send(c_send.at[g, pl.ds(0, n)], c_recv.at[g, pl.ds(0, n)], c_s.at[g], c_r.at[g], partner))
-
-    plane_copies = [[], []]
-    for g in range(2):
-        mine = mean(g * 2 + core)
+        core_copies.append(send(c_send.at[g, 1 - core, pl.ds(0, n)], c_recv.at[g, pl.ds(0, n)], c_s.at[g], c_r.at[g], partner))
+
+    for g in range(4):
         core_copies[g].wait()
-        mine += c_recv[g, :64].reshape(16, 4, 16, 128)
+        mine = (c_send[g, core, :32] + c_recv[g, :32]).reshape(16, 2, 16, 128)
         own[g] = mine
-        p_send, p_recv = (p_send0, p_recv0) if g == 0 else (p_send1, p_recv1)
-        p_send[:, :4] = mine.astype(BF16)
         if g == 0:
-            q += c_recv[0, 64, :8]
-            p_send[:, 4] = jnp.broadcast_to(split_q(q)[None], (16, 16, 128))
+            p_send0[:, :2] = mine.astype(BF16)
+            q += c_recv[0, 32, :8]
+            p_send0[:, 2] = jnp.broadcast_to(split_q(q)[None], (16, 16, 128))
+        else:
+            p_send[g - 1] = mine.astype(BF16)
         for k, (dx, dy) in enumerate(PLANE):
             to = ((x + dx) % 4) * 4 + (y + dy) % 4
-            plane_copies[g].append(send(p_send.at[to], p_recv.at[k], p_s.at[g, k], p_r.at[g, k], plane_peers[k]))
-
-    z_copies = [[], []]
-    for g in range(2):
-        p_recv = p_recv0 if g == 0 else p_recv1
+            src, dst = (p_send0.at[to], p_recv0.at[k]) if g == 0 else (p_send.at[g - 1, to], p_recv.at[g - 1, k])
+            send(src, dst, p_s.at[g], p_r.at[g], plane_peers[k])
+
+    for g in range(4):
         total = own[g, plane]
+        wait_all(p_recv0 if g == 0 else p_recv.at[g - 1], p_s.at[g], p_r.at[g], plane_peers[0])
         for k in range(15):
-            plane_copies[g][k].wait()
-            total += p_recv[k, :4].astype(F32)
             if g == 0:
-                q += join_q(p_recv[k, 4])
+                total += p_recv0[k, :2].astype(F32)
+                q += join_q(p_recv0[k, 2])
+            else:
+                total += p_recv[g - 1, k].astype(F32)
         z_own[g] = total
-        z_send[g, :4] = total.astype(BF16)
+        z_send[g, :2] = total.astype(BF16)
         if g == 0:
-            z_send[0, 4] = split_q(q)
-        n = 5 if g == 0 else 4
+            z_send[0, 2] = split_q(q)
         for k in range(7):
-            z_copies[g].append(send(z_send.at[g, pl.ds(0, n)], z_recv.at[g, k, pl.ds(0, n)], z_s.at[g, k], z_r.at[g, k], z_peers[k]))
-
+            src, dst = (z_send.at[0], z_recv0.at[k]) if g == 0 else (z_send.at[g, pl.ds(0, 2)], z_recv.at[g - 1, k])
+            send(src, dst, z_s.at[g], z_r.at[g], z_peers[k])
+
+    b_copy.wait()
+    m_copy.wait()
     row = lax.broadcasted_iota(jnp.int32, (8, 128), 0)
-    pick_row = lax.broadcasted_iota(jnp.int32, (16, 128), 0) + (plane % 8) * 16
+    pick_row = lax.broadcasted_iota(jnp.int32, (16, 128), 0) + (plane // 2) * 16
     pick = lax.broadcasted_iota(jnp.int32, (16, 128), 1) == pick_row
-    gather_copies = [[], []]
-    for g in range(2):
+    for g in range(4):
         total = z_own[g]
+        wait_all(z_recv0 if g == 0 else z_recv.at[g - 1], z_s.at[g], z_r.at[g], z_peers[0])
         for k in range(7):
-            z_copies[g][k].wait()
-            total += z_recv[g, k, :4].astype(F32)
             if g == 0:
-                q += join_q(z_recv[0, k, 4])
+                total += z_recv0[k, :2].astype(F32)
+                q += join_q(z_recv0[k, 2])
+            else:
+                total += z_recv[g - 1, k].astype(F32)
         if g == 0:
             precision = q + 1.0 / PRIOR_VAR
-        line = jnp.sum(jnp.where(row == (g * 2 + core) * 2 + plane // 8, precision, 0.0), axis=0, keepdims=True)
+        line = jnp.sum(jnp.where(row == g * 2 + core, precision, 0.0), axis=0, keepdims=True)
         column = jnp.sum(jnp.where(pick, line, 0.0), axis=1, keepdims=True)
-        spot = (g * 2 + core) * 16 + plane
-        coef[spot] = (total / column).astype(BF16)
+        spot = coef.at[(g * 2 + core) * 8 + plane // 2, pl.ds((plane % 2) * 2, 2)]
+        coef[(g * 2 + core) * 8 + plane // 2, pl.ds((plane % 2) * 2, 2)] = (total / column).astype(BF16)
         for k in range(15):
-            gather_copies[g].append(send(coef.at[spot], coef.at[spot], g_s.at[g, k], g_r.at[g, k], plane_peers[k]))
-
-    b_copy.wait()
-    m_copy.wait()
-
-    def field(block):
-        c = rows_of(coef[pl.ds(block * 16, 16)])
-        rows = pl.ds(pl.multiple_of(block * TB, TB), TB)
-        out_ref[rows, :] = (jnp.dot(c, basis_v[...], preferred_element_type=F32) + clim_ref[...]).astype(BF16)
+            send(spot, spot, g_s.at[g], g_r.at[g], plane_peers[k])
+
+    def field(g):
+        c = rows_of(coef[g * 16 : g * 16 + 16])
+        out_ref[g * 256 : g * 256 + 256, :] = (jnp.dot(c, basis_v[...], preferred_element_type=F32) + clim_ref[...]).astype(BF16)
 
     last = []
-    for g in range(2):
-        for k in range(15):
-            gather_copies[g][k].wait()
-        half = coef.at[pl.ds((g * 2 + core) * 16, 16)]
+    for g in range(4):
+        wait_all(p_recv.at[0], g_s.at[g], g_r.at[g], plane_peers[0])
+        half = coef.at[pl.ds((g * 2 + core) * 8, 8)]
         last.append(send(half, half, h_s.at[g], h_r.at[g], partner))
-    field(core)
-    last[0].wait()
-    field(1 - core)
-    field(2 + core)
-    last[1].wait()
-    field(3 - core)
+    for g in range(3):
+        last[g].wait()
+    for g in range(3):
+        field(g)
+    last[3].wait()
+    field(3)
 
 
 VM = pl.BlockSpec(memory_space=pltpu.VMEM)
@@ -290,10 +296,9 @@
             pltpu.VMEM((1024, 512), F32), pltpu.VMEM((1024, 512), BF16), pltpu.VMEM((512, 1024), BF16), pltpu.VMEM((1, 1024), F32),
             pltpu.VMEM((1024, 1024), BF16), pltpu.VMEM((1024, 1024), BF16),
             pltpu.VMEM((1024, 1), F32), pltpu.VMEM((8, 128), F32),
-            tile32(2, 65), tile32(2, 65), tile32(2, 16, 4),
-            tile(16, 5), tile(16, 4), tile(15, 5), tile(15, 4), tile(2, 5), tile(2, 7, 5), tile32(2, 4), tile(64, 4),
-            dma((3,)), dma((4,)), dma, dma, dma, dma((2,)), dma((2,)), dma((2, 15)), dma((2, 15)), dma((2, 7)), dma((2, 7)),
-            dma((2, 15)), dma((2, 15)), dma((2,)), dma((2,)),
+            tile32(4, 2, 33), tile32(4, 33), tile32(4, 16, 2),
+            tile(16, 3), tile(3, 16, 2), tile(15, 3), tile(3, 15, 2), tile(4, 3), tile(7, 3), tile(3, 7, 2), tile32(4, 2), tile(64, 4),
+            dma((3,)), dma((4,)), dma, dma, dma, dma((4,)), dma((4,)), *[dma((4,))] * 8,
         ],
         compiler_params=pltpu.CompilerParams(collective_id=0, has_side_effects=True, vmem_limit_bytes=44 << 20),
     )(*[pltpu.with_memory_space_constraint(a, pltpu.HBM) for a in arrays])

time: 45.4 us -> 40.2 us (0.89)
  Pallas kernels: 44 us -> 38.8 us
    pallas_call x1, Pallas kernels: 44 us -> 38.8 us  [body(): pl.pallas_call(main_kernel, out_shape=jax.ShapeDtypeStruct((1024, 1024),...]
where the time goes in v3:
time: 40.2 us; the launch traced here: 40.1 us
  Pallas kernels  38.8 us (97%)
  local copies, waits for them, and re-layouts  1.32 us (3%)
    pallas_call x1, Pallas kernels, body(): pl.pallas_call(main_kernel, out_shape=jax.ShapeDtypeStruct((1024, 1024),...  38.8 us
    unnamed x1, local copies, waits for them, and re-layouts  1.32 us

profile of v3, /device:TPU:1, one launch (start us, length us, event | category | flops | bytes accessed | tf_op | source)
XLA Modules:
  0.0 40.1 jit_solution(5428010596702405549)
XLA Ops:
  0.0 38.8 %shard_map.73 = bf16[1024,1024]{1,0:T(8,128)(2,1)S(1)} custom-call(f32[16,1024]{1,0:T(8,128)} %bitcast.7, f32[16,4096]{1,0:T(8,128)} %cand_hbm.1, s32[8,128]{1,0:T(8,128)} %bitcast.8, f32[1024,1024]{1,0:T(8,128)} %bitcast.5, f32[1024,512]{1,0:T(8,128)} %bitcast.6, bf16[512,1024]{1,0:T(8,128)(2,1)} %basis_ref.1, f32[1,1024]{1,0:T(1,128)} %bitcast.9), custom_call_target="tpu_custom_call" | custom-call | tf_op jit(solution)/shard_map/pallas_call | solution.py:287
  38.8 1.3 %copy.9 = bf16[1024,1024]{1,0:T(8,128)(2,1)} copy(bf16[1024,1024]{1,0:T(8,128)(2,1)S(1)} %shard_map.73) | data formatting | bytes 4194304

commit v4 on v3

--- a/solution.py
+++ b/solution.py
@@ -8,7 +8,7 @@
 from jax.sharding import PartitionSpec as P
 
 MESH = pl.DeviceIdType.MESH
-F32, BF16 = jnp.float32, jnp.bfloat16
+F32, BF16, F8 = jnp.float32, jnp.bfloat16, jnp.float8_e4m3fn
 PRIOR_VAR = 1.1
 NK = 2
 PLANE = [(dx, dy) for dx in range(4) for dy in range(4) if dx or dy]
@@ -91,7 +91,7 @@
 
 
 def main_kernel(train_hbm, cand_hbm, ids_hbm, factor_ref, weights_ref, basis_ref, clim_hbm, out_ref,
-                train_ref, cand_ref, ids_ref, query_ref, left_ref, right_ref, lf, lb, ll, wf, wb, basis_v, clim_ref, kh, kl, term_ref, q_ref,
+                train_ref, cand_ref, ids_ref, query_ref, left_ref, right_ref, lf, lb, l8, wf, wb, basis_v, clim_ref, kh, k8, term_ref, q_ref,
                 c_send, c_recv, own, p_send0, p_send, p_recv0, p_recv, z_send, z_recv0, z_recv, z_own, coef,
                 i_sem, l_sem, w_sem, b_sem, m_sem, c_s, c_r, p_s, p_r, z_s, z_r, g_s, g_r, h_s, h_r):
     y_lo, z, x, y_hi, core = place()
@@ -148,7 +148,11 @@
         kernel = jnp.exp(jnp.dot(left_ref[rows, :], right_ref[...], preferred_element_type=F32))
         high = kernel.astype(BF16)
         kh[rows, :] = high
-        kl[rows, :] = (kernel - high.astype(F32)).astype(BF16)
+        low = ((kernel - high.astype(F32)) * 4096.0).astype(F8)
+        top = (kernel * 16.0).astype(F8)
+        for i in range(4):
+            k8[rows, i * 512 : i * 512 + 256] = low[:, i * 256 : i * 256 + 256]
+            k8[rows, i * 512 + 256 : i * 512 + 512] = top[:, i * 256 : i * 256 + 256]
 
     def explain(tb):
         rows = slice(tb * 256, tb * 256 + 256)
@@ -156,8 +160,7 @@
         for b in range(4):
             block = slice(b * 256, b * 256 + 256), slice(0, 256 * (b + 1))
             whitened = dot_nt(kh[rows, block[1]], lb[block])
-            whitened += dot_nt(kl[rows, block[1]], lb[block])
-            whitened += dot_nt(kh[rows, block[1]], ll[block])
+            whitened += dot_nt(k8[rows, : 512 * (b + 1)], l8[block[0], : 512 * (b + 1)]) * 2.0**-15
             squares += whitened[:, :128] * whitened[:, :128] + whitened[:, 128:] * whitened[:, 128:]
         explained = jnp.sum(squares, axis=1, keepdims=True)
         post_var = PRIOR_VAR - explained
@@ -179,7 +182,11 @@
         factor = lf[block]
         high = factor.astype(BF16)
         lb[block] = high
-        ll[block] = (factor - high.astype(F32)).astype(BF16)
+        low = ((factor - high.astype(F32)) * 2048.0).astype(F8)
+        top = (factor * 8.0).astype(F8)
+        for i in range(b + 1):
+            l8[block[0], i * 512 : i * 512 + 256] = top[:, i * 256 : i * 256 + 256]
+            l8[block[0], i * 512 + 256 : i * 512 + 512] = low[:, i * 256 : i * 256 + 256]
     for tb in range(4):
         if tb + NK < 4:
             cross(tb + NK)
@@ -292,9 +299,9 @@
         scratch_shapes=[
             pltpu.VMEM((16, 1024), F32), pltpu.VMEM((16, 4096), F32), pltpu.VMEM((8, 128), jnp.int32), pltpu.VMEM((16, 1024), F32),
             pltpu.VMEM((1024, 128), BF16), pltpu.VMEM((128, 1024), BF16),
-            pltpu.VMEM((1024, 1024), F32), pltpu.VMEM((1024, 1024), BF16), pltpu.VMEM((1024, 1024), BF16),
+            pltpu.VMEM((1024, 1024), F32), pltpu.VMEM((1024, 1024), BF16), pltpu.VMEM((1024, 2048), F8),
             pltpu.VMEM((1024, 512), F32), pltpu.VMEM((1024, 512), BF16), pltpu.VMEM((512, 1024), BF16), pltpu.VMEM((1, 1024), F32),
-            pltpu.VMEM((1024, 1024), BF16), pltpu.VMEM((1024, 1024), BF16),
+            pltpu.VMEM((1024, 1024), BF16), pltpu.VMEM((1024, 2048), F8),
             pltpu.VMEM((1024, 1), F32), pltpu.VMEM((8, 128), F32),
             tile32(4, 2, 33), tile32(4, 33), tile32(4, 16, 2),
             tile(16, 3), tile(3, 16, 2), tile(15, 3), tile(3, 15, 2), tile(4, 3), tile(7, 3), tile(3, 7, 2), tile32(4, 2), tile(64, 4),

time: 40.2 us -> 38.8 us (0.965)
  Pallas kernels: 38.8 us -> 37.3 us
    pallas_call x1, Pallas kernels: 38.8 us -> 37.3 us  [body(): pl.pallas_call(main_kernel, out_shape=jax.ShapeDtypeStruct((1024, 1024),...]
where the time goes in v4:
time: 38.8 us; the launch traced here: 38.7 us
  Pallas kernels  37.3 us (96%)
  local copies, waits for them, and re-layouts  1.32 us (3%)
    pallas_call x1, Pallas kernels, body(): pl.pallas_call(main_kernel, out_shape=jax.ShapeDtypeStruct((1024, 1024),...  37.3 us
    unnamed x1, local copies, waits for them, and re-layouts  1.32 us

profile of v4, /device:TPU:1, one launch (start us, length us, event | category | flops | bytes accessed | tf_op | source)
XLA Modules:
  0.0 38.7 jit_solution(17815753081693887233)
XLA Ops:
  0.0 37.3 %shard_map.73 = bf16[1024,1024]{1,0:T(8,128)(2,1)S(1)} custom-call(f32[16,1024]{1,0:T(8,128)} %bitcast.7, f32[16,4096]{1,0:T(8,128)} %cand_hbm.1, s32[8,128]{1,0:T(8,128)} %bitcast.8, f32[1024,1024]{1,0:T(8,128)} %bitcast.5, f32[1024,512]{1,0:T(8,128)} %bitcast.6, bf16[512,1024]{1,0:T(8,128)(2,1)} %basis_ref.1, f32[1,1024]{1,0:T(1,128)} %bitcast.9), custom_call_target="tpu_custom_call" | custom-call | tf_op jit(solution)/shard_map/pallas_call | solution.py:294
  37.3 1.3 %copy.9 = bf16[1024,1024]{1,0:T(8,128)(2,1)} copy(bf16[1024,1024]{1,0:T(8,128)(2,1)S(1)} %shard_map.73) | data formatting | bytes 4194304

commit v5 on v4

--- a/solution.py
+++ b/solution.py
@@ -130,10 +130,14 @@
         copy.start()
         return copy
 
+    sent = []
+
     def wait_all(like, s_sem, r_sem, peer):
-        pltpu.make_async_remote_copy(
+        copy = pltpu.make_async_remote_copy(
             src_ref=like, dst_ref=like, send_sem=s_sem, recv_sem=r_sem, device_id=peer, device_id_type=MESH
-        ).wait()
+        )
+        copy.wait_recv()
+        sent.append(copy)
 
     for copy in copies:
         copy.wait()
@@ -211,7 +215,8 @@
         core_copies.append(send(c_send.at[g, 1 - core, pl.ds(0, n)], c_recv.at[g, pl.ds(0, n)], c_s.at[g], c_r.at[g], partner))
 
     for g in range(4):
-        core_copies[g].wait()
+        core_copies[g].wait_recv()
+        sent.append(core_copies[g])
         mine = (c_send[g, core, :32] + c_recv[g, :32]).reshape(16, 2, 16, 128)
         own[g] = mine
         if g == 0:
@@ -280,6 +285,8 @@
         field(g)
     last[3].wait()
     field(3)
+    for copy in sent:
+        copy.wait_send()
 
 
 VM = pl.BlockSpec(memory_space=pltpu.VMEM)

time: 38.8 us -> 38.9 us (level)
  no operation moved by 1% of the time
where the time goes in v5:
time: 38.9 us; the launch traced here: 38.8 us
  Pallas kernels  37.4 us (96%)
  local copies, waits for them, and re-layouts  1.32 us (3%)
    pallas_call x1, Pallas kernels, body(): pl.pallas_call(main_kernel, out_shape=jax.ShapeDtypeStruct((1024, 1024),...  37.4 us
    unnamed x1, local copies, waits for them, and re-layouts  1.32 us

profile of v5, /device:TPU:1, one launch (start us, length us, event | category | flops | bytes accessed | tf_op | source)
XLA Modules:
  0.0 38.8 jit_solution(9611060801900548413)
XLA Ops:
  0.0 37.4 %shard_map.73 = bf16[1024,1024]{1,0:T(8,128)(2,1)S(1)} custom-call(f32[16,1024]{1,0:T(8,128)} %bitcast.7, f32[16,4096]{1,0:T(8,128)} %cand_hbm.1, s32[8,128]{1,0:T(8,128)} %bitcast.8, f32[1024,1024]{1,0:T(8,128)} %bitcast.5, f32[1024,512]{1,0:T(8,128)} %bitcast.6, bf16[512,1024]{1,0:T(8,128)(2,1)} %basis_ref.1, f32[1,1024]{1,0:T(1,128)} %bitcast.9), custom_call_target="tpu_custom_call" | custom-call | tf_op jit(solution)/shard_map/pallas_call | solution.py:301
  37.5 1.3 %copy.9 = bf16[1024,1024]{1,0:T(8,128)(2,1)} copy(bf16[1024,1024]{1,0:T(8,128)(2,1)S(1)} %shard_map.73) | data formatting | bytes 4194304
